TPU v7x, 32 devices: a whole 2x2x4 slice. The times are simulated.
32 devices in a mesh: gx: 8 (over y, x, core), gy: 4 (over z).
Axes of the slice: x: 2, y: 2, z: 4, core: 2. Of those that a mesh axis runs over, the one named last changes fastest.
Arguments:
- velocity: float32 [64, 32, 128], P('gx', 'gy'), may hold values from -6 to 6
- cotangent: float32 [64, 32, 128], P('gx', 'gy'), may hold values from -6 to 6
- block_ids: int32 [8, 4, 128], P('gx', 'gy'), may hold values from 0 to 127, as said below
- fluid_count: int32 [8, 4], P('gx', 'gy'), may hold values from 32 to 128, as said below
- fluid_cells: int32 [8, 4, 8192], P('gx', 'gy'), may hold values 0 or 1
- w_in: bfloat16 [64, 7], replicated, may hold values from -2 to 2
- w_mid: bfloat16 [64, 64], replicated, may hold values from -0.75 to 0.75
- w_out: bfloat16 [1, 64], replicated, may hold values from -0.75 to 0.75
Outputs:
- new_field: float32 [64, 32, 128], P('gx', 'gy')
- grad_field: float32 [64, 32, 128], P('gx', 'gy')
- grad_in: float32 [64, 7], replicated
- grad_mid: float32 [64, 64], replicated
- grad_out: float32 [1, 64], replicated
Inputs may be any that keep to these rules, and one draw needn't show every extreme that they name: `block_ids`: within one device's list the block numbers are distinct. `fluid_count`: some device's list is wholly live.
All inputs are finite; a program needn't handle non-finite values. No bound on the sum of `fluid_cells` on one device may be relied on, other than what follows from the above.
Results may differ from a plain program's by a relative error of at most 0.018.
Values sent between devices are 32-bit elements; how exact they have to be, the bound alone decides.
A program may use at most 64 MiB of HBM per device.

v0:
```python
import jax
import jax.numpy as jnp
from jax import lax
from jax.sharding import PartitionSpec as P

viscosity = 0.1


def padded_2(cells, sides, width):
    for axis, dim in sides:
        count = lax.axis_size(axis)
        head = lax.slice_in_dim(cells, 0, width, axis=dim)
        tail = lax.slice_in_dim(cells, cells.shape[dim] - width, cells.shape[dim], axis=dim)
        cells = jnp.concatenate(
            [
                lax.ppermute(tail, axis, [(i, (i + 1) % count) for i in range(count)]),
                cells,
                lax.ppermute(head, axis, [((i + 1) % count, i) for i in range(count)]),
            ],
            axis=dim,
        )
    return cells


def to_blocks(field):
    lead = field.shape[:-3]
    sizex, sizey, sizez = field.shape[-3:]
    count = len(lead)
    shaped = field.reshape(lead + (sizex // 4, 4, sizey // 4, 4, sizez // 4, 4))
    order = list(range(count)) + [count, count + 2, count + 4, count + 1, count + 3, count + 5]
    return shaped.transpose(order).reshape(lead + (sizex * sizey * sizez // 64, 64))


def from_blocks(blocks, sizex, sizey, sizez):
    lead = blocks.shape[:-2]
    count = len(lead)
    shaped = blocks.reshape(lead + (sizex // 4, sizey // 4, sizez // 4, 4, 4, 4))
    order = list(range(count)) + [count, count + 3, count + 1, count + 4, count + 2, count + 5]
    return shaped.transpose(order).reshape(lead + (sizex, sizey, sizez))


def closure_tile(padded, cotile, ids, count, fluid, w_in, w_mid, w_out):
    sizex = padded.shape[0] - 2
    sizey = padded.shape[1] - 2
    sizez = padded.shape[2]
    slots = ids.shape[0]
    nblocks = sizex * sizey * sizez // 64
    center = padded[1:-1, 1:-1]
    stencil = jnp.stack(
        [
            center,
            padded[2:, 1:-1],
            padded[:-2, 1:-1],
            padded[1:-1, 2:],
            padded[1:-1, :-2],
            jnp.roll(center, -1, 2),
            jnp.roll(center, 1, 2),
        ]
    ).astype(jnp.bfloat16)
    chosen = jnp.take(to_blocks(stencil), ids, axis=1).reshape(7, slots * 64)
    live = (jnp.arange(slots) < count).astype(jnp.float32)
    weight = (fluid.reshape(slots, 64).astype(jnp.float32) * live[:, None]).reshape(slots * 64)
    h1 = jnp.tanh(jnp.dot(w_in, chosen, preferred_element_type=jnp.float32)).astype(jnp.bfloat16)
    h2 = jnp.tanh(jnp.dot(w_mid, h1, preferred_element_type=jnp.float32)).astype(jnp.bfloat16)
    closure = jnp.dot(w_out, h2, preferred_element_type=jnp.float32)[0] * weight
    corr_blocks = jnp.zeros((nblocks, 64), jnp.float32).at[ids].add(closure.reshape(slots, 64))
    corr = from_blocks(corr_blocks, sizex, sizey, sizez)
    cot_sel = jnp.take(to_blocks(cotile), ids, axis=0).reshape(slots * 64)
    dcl = (cot_sel * weight).astype(jnp.bfloat16)
    h2f = h2.astype(jnp.float32)
    h1f = h1.astype(jnp.float32)
    dh2 = jnp.dot(w_out.T, dcl[None, :], preferred_element_type=jnp.float32)
    da2 = (dh2 * (1.0 - h2f * h2f)).astype(jnp.bfloat16)
    dh1 = jnp.dot(w_mid.T, da2, preferred_element_type=jnp.float32)
    da1 = (dh1 * (1.0 - h1f * h1f)).astype(jnp.bfloat16)
    dfeat = jnp.dot(w_in.T, da1, preferred_element_type=jnp.float32)
    dims = (((1,), (1,)), ((), ()))
    gin = lax.dot_general(da1, chosen, dims, preferred_element_type=jnp.float32)
    gmid = lax.dot_general(da2, h1, dims, preferred_element_type=jnp.float32)
    gout = lax.dot_general(dcl[None, :], h2, dims, preferred_element_type=jnp.float32)
    dense = jnp.zeros((7, nblocks, 64), jnp.float32).at[:, ids].add(dfeat.reshape(7, slots, 64))
    dense = from_blocks(dense, sizex, sizey, sizez)
    local = dense[0] + jnp.roll(dense[5], 1, 2) + jnp.roll(dense[6], -1, 2)
    return (corr, local, dense[1:5], gin, gmid, gout)


def padded_laplace(padded):
    center = padded[1:-1, 1:-1]
    total = padded[2:, 1:-1] + padded[:-2, 1:-1] + padded[1:-1, 2:] + padded[1:-1, :-2]
    total = total + jnp.roll(center, -1, 2) + jnp.roll(center, 1, 2)
    return total - 6.0 * center


def body(velocity, cotangent, block_ids, fluid_count, fluid_cells, w_in, w_mid, w_out):
    slots = block_ids.shape[2]
    both = padded_2(jnp.stack([velocity, cotangent]), (("gx", 1), ("gy", 2)), 1)
    padded = both[0]
    cot_pad = both[1]
    corr, local, side, gin, gmid, gout = closure_tile(
        padded,
        cotangent,
        block_ids.reshape(slots),
        fluid_count[0, 0],
        fluid_cells.reshape(slots * 64),
        w_in,
        w_mid,
        w_out,
    )
    new_field = velocity + viscosity * padded_laplace(padded) + corr
    beside_all = padded_2(side, (("gx", 1), ("gy", 2)), 1)
    beside = (
        beside_all[0, :-2, 1:-1]
        + beside_all[1, 2:, 1:-1]
        + beside_all[2, 1:-1, :-2]
        + beside_all[3, 1:-1, 2:]
    )
    grad_field = cotangent + viscosity * padded_laplace(cot_pad) + local + beside
    flat = jnp.concatenate([gin.reshape(-1), gmid.reshape(-1), gout.reshape(-1)])
    total = lax.psum(flat, ("gx", "gy"))
    scale = 1.0 / jnp.sqrt(jnp.float32(lax.axis_size("gx") * lax.axis_size("gy") * slots * 64))
    total = total * scale
    width = gmid.shape[0]
    grad_in = total[: width * 7].reshape(width, 7)
    grad_mid = total[width * 7 : width * 7 + width * width].reshape(width, width)
    grad_out = total[width * 7 + width * width :].reshape(1, width)
    return (new_field, grad_field, grad_in, grad_mid, grad_out)


def solution(mesh):
    in_specs = (
        P("gx", "gy", None),
        P("gx", "gy", None),
        P("gx", "gy", None),
        P("gx", "gy"),
        P("gx", "gy", None),
        P(),
        P(),
        P(),
    )
    out_specs = (P("gx", "gy", None), P("gx", "gy", None), P(), P(), P())
    return jax.shard_map(body, mesh=mesh, in_specs=in_specs, out_specs=out_specs, check_vma=False)
```

profile of v0, /device:TPU:0, one launch (start us, length us, event | category | flops | bytes accessed | tf_op | source)
XLA Modules:
  0.0 119.6 jit_solution(2853110013341421377)
XLA Ops:
  1.9 2.9 %collective-permute-start.1 = (f32[2,1,8,128]{3,2,1,0:T(8,128)S(1)}, f32[2,1,8,128]{3,2,1,0:T(8,128)S(1)}, u32[]{:S(2)}, u32[]{:S(2)}) collective-permute-start(f32[2,1,8,128]{3,2,1,0:T(8,128)S(1)} %get-tuple-element.45), channel_id=1, source_target_pairs={{4,0},{8,4},{12,8},{16,12},{20,16},{24,20},{28,24},{0,28},{5,1},{9... | collective-permute-start | bytes 24584 | tf_op jit(solution)/shard_map/ppermute | solution.py:18
  4.8 0.8 convert_reduce_fusion
  6.4 1.8 %reshape.198 = f32[2,4,2,4,32,4]{5,4,3,2,1,0:T(8,128)S(1)} reshape(f32[8,8,128]{2,1,0:T(8,128)} %param.9) | data formatting | bytes 65536 | tf_op jit(solution)/shard_map/reshape | solution.py:29
  12.3 2.4 %collective-permute-start.2 = (f32[2,10,1,128]{3,2,1,0:T(1,128)S(1)}, f32[2,10,1,128]{3,2,1,0:T(1,128)S(1)}, u32[]{:S(2)}, u32[]{:S(2)}) collective-permute-start(f32[2,10,1,128]{3,2,1,0:T(1,128)S(1)} %get-tuple-element.42), channel_id=1, source_target_pairs={{0,1},{1,2},{2,3},{3,0},{4,5},{5,6},{6,7},{7,4},{8,9},{9,10},{10,1... | collective-permute-start | bytes 30728 | tf_op jit(solution)/shard_map/ppermute | solution.py:16
  14.7 2.1 %collective-permute-start.3 = (f32[2,10,1,128]{3,2,1,0:T(1,128)S(1)}, f32[2,10,1,128]{3,2,1,0:T(1,128)S(1)}, u32[]{:S(2)}, u32[]{:S(2)}) collective-permute-start(f32[2,10,1,128]{3,2,1,0:T(1,128)S(1)} %get-tuple-element.43), channel_id=1, source_target_pairs={{1,0},{2,1},{3,2},{0,3},{5,4},{6,5},{7,6},{4,7},{9,8},{10,9},{11,1... | collective-permute-start | bytes 30728 | tf_op jit(solution)/shard_map/ppermute | solution.py:18
  17.5 1.0 collective-permute-done.2
  20.1 1.1 stack.40
  21.8 1.1 stack.42
  23.4 1.1 stack.36
  25.1 1.1 stack.39
  26.6 1.1 stack.38
  28.2 1.1 stack.37
  29.8 1.1 stack.41
  34.5 1.3 %fusion.11 = f32[64,64]{1,0:T(8,128)} fusion(bf16[8192,64]{0,1:T(8,128)(2,1)S(1)} %fusion, bf16[8192,64]{0,1:T(8,128)(2,1)S(1)} %fusion.1, f32[64]{0:T(128)S(1)} %bitcast_convert_fusion, f32[8192]{0:T(1024)S(1)} %reshape.207), kind=kOutput, calls=%fused_computation.27 | convolution fusion | flops 70254592 | bytes 2146560 | tf_op jit(solution)/shard_map/dot_general | solution.py:79
  35.8 0.8 fusion.2
  36.6 1.0 fusion.5
  38.4 5.1 %scatter_fusion = f32[7,128,64]{2,0,1:T(8,128)S(1)} fusion(f32[7,128,64]{2,0,1:T(8,128)S(1)} %broadcast_in_dim.40, s32[128]{0:T(128)S(1)} %fusion.31, f32[128,7,64]{2,1,0:T(8,128)S(1)} %copy.62), kind=kCustom, calls=%fused_computation.3 | custom fusion | flops 57344 | bytes 688640 | tf_op jit(solution)/shard_map/scatter-add | solution.py:81
  44.4 0.9 fusion.36
  45.3 1.0 slice.246
  46.3 2.3 %dot_general.41 = bf16[128,64,64]{1,0,2:T(8,128)(2,1)S(1)} reshape(bf16[8192,64]{0,1:T(8,128)(2,1)S(1)} %fusion.1) | data formatting | bytes 2097152 | tf_op jit(solution)/shard_map/dot_general | solution.py:65
  48.6 1.7 %convolution_bitcast_fusion.1 = f32[64]{0:T(128)} fusion(bf16[8192,1]{0,1:T(2,128)(2,1)} %reshape.242, bf16[8192,64]{0,1:T(8,128)(2,1)S(1)} %fusion.1), kind=kOutput, calls=%fused_computation.14 | convolution fusion | flops 1048576 | bytes 1065216 | tf_op jit(solution)/shard_map/dot_general | solution.py:80
  50.2 0.9 reshape.203
  51.1 0.8 reshape.204
  52.7 39.6 %psum.7 = f32[4608]{0:T(1024)S(1)} all-reduce(f32[4608]{0:T(1024)S(1)} %concatenate.62), channel_id=1, replica_groups=mesh['gx'=8,'gy'=4] {'gx','gy'}, use_global_device_ids=true, to_apply=%region_2.3 | all-reduce | flops 4608 | bytes 36864 | tf_op jit(solution)/shard_map/psum | solution.py:119
  92.3 1.3 %multiply_reduce_fusion = f32[128,64]{1,0:T(8,128)S(1)} fusion(f32[64]{0:T(128)} %copy-done.23, bf16[128,64,64]{1,0,2:T(8,128)(2,1)S(1)} %dot_general.41), kind=kLoop, calls=%fused_computation.11 | loop fusion | flops 1564672 | bytes 1081600 | tf_op jit(solution)/shard_map/dot_general | solution.py:65
  93.6 1.4 %scatter_custom_fusion = f32[128,64]{1,0:T(8,128)S(1)} fusion(s32[128]{0:T(128)} %copy-done.22, f32[128,64]{1,0:T(8,128)S(1)} %multiply_reduce_fusion, f32[128,64]{1,0:T(8,128)S(1)} %convert_element_type.72, f32[128]{0:T(128)S(1)} %copy-done.21, f32[]{:T(128)} %constant.20.clone.1), kind=kCustom, calls=%fused_computation.22 | custom fusion | flops 24576 | bytes 99328 | tf_op jit(solution)/shard_map/scatter-add | solution.py:66
  97.1 3.0 %copy.67 = f32[4,2,4,2,4,32,4]{6,5,4,3,2,1,0:T(8,128)} copy(f32[4,2,4,2,4,32,4]{5,3,1,6,4,2,0:T(2,128)S(1)} %copy-done.1) | data formatting | bytes 262144 | tf_op jit(solution)/shard_map/slice | solution.py:84
  100.1 4.9 %slice.202 = f32[4,8,8,128]{3,2,1,0:T(8,128)S(1)} reshape(f32[4,2,4,2,4,32,4]{6,5,4,3,2,1,0:T(8,128)} %copy.67) | data formatting | bytes 262144 | tf_op jit(solution)/shard_map/slice | solution.py:84
  105.1 2.6 %collective-permute-start.5 = (f32[4,1,8,128]{3,2,1,0:T(8,128)S(1)}, f32[4,1,8,128]{3,2,1,0:T(8,128)S(1)}, u32[]{:S(2)}, u32[]{:S(2)}) collective-permute-start(f32[4,1,8,128]{3,2,1,0:T(8,128)S(1)} %get-tuple-element.27), channel_id=1, source_target_pairs={{4,0},{8,4},{12,8},{16,12},{20,16},{24,20},{28,24},{0,28},{5,1},{9... | collective-permute-start | bytes 49160 | tf_op jit(solution)/shard_map/ppermute | solution.py:18
  107.7 1.4 %collective-permute-done.4 = f32[4,1,8,128]{3,2,1,0:T(8,128)S(1)} collective-permute-done((f32[4,1,8,128]{3,2,1,0:T(8,128)S(1)}, f32[4,1,8,128]{3,2,1,0:T(8,128)S(1)}, u32[]{:S(2)}, u32[]{:S(2)}) %collective-permute-start.4) | collective-permute-done | bytes 16416 | tf_op jit(solution)/shard_map/ppermute | solution.py:16
  109.2 2.1 %collective-permute-start.6 = (f32[4,10,1,128]{3,2,1,0:T(1,128)S(1)}, f32[4,10,1,128]{3,2,1,0:T(1,128)S(1)}, u32[]{:S(2)}, u32[]{:S(2)}) collective-permute-start(f32[4,10,1,128]{3,2,1,0:T(1,128)S(1)} %get-tuple-element.25), channel_id=1, source_target_pairs={{0,1},{1,2},{2,3},{3,0},{4,5},{5,6},{6,7},{7,4},{8,9},{9,10},{10,1... | collective-permute-start | bytes 61448 | tf_op jit(solution)/shard_map/ppermute | solution.py:16
  111.3 1.8 %collective-permute-start.7 = (f32[4,10,1,128]{3,2,1,0:T(1,128)S(1)}, f32[4,10,1,128]{3,2,1,0:T(1,128)S(1)}, u32[]{:S(2)}, u32[]{:S(2)}) collective-permute-start(f32[4,10,1,128]{3,2,1,0:T(1,128)S(1)} %get-tuple-element.26), channel_id=1, source_target_pairs={{1,0},{2,1},{3,2},{0,3},{5,4},{6,5},{7,6},{4,7},{9,8},{10,9},{11,1... | collective-permute-start | bytes 61448 | tf_op jit(solution)/shard_map/ppermute | solution.py:18
  (142 shorter events, 24.8 us)
Async XLA Ops:
  0.6 33.4 %copy-start = (bf16[64,64]{1,0:T(8,128)(2,1)S(1)}, bf16[64,64]{1,0:T(8,128)(2,1)}, u32[]{:S(2)}) copy-start(bf16[64,64]{1,0:T(8,128)(2,1)} %param.14) | copy-start | bytes 24580
  0.6 11.6 %copy-start.2 = (f32[8,8,128]{2,1,0:T(8,128)S(1)}, f32[8,8,128]{2,1,0:T(8,128)}, u32[]{:S(2)}) copy-start(f32[8,8,128]{2,1,0:T(8,128)} %param.9) | copy-start | bytes 98308
  0.7 11.6 %copy-start.5 = (f32[8,8,128]{2,1,0:T(8,128)S(1)}, f32[8,8,128]{2,1,0:T(8,128)}, u32[]{:S(2)}) copy-start(f32[8,8,128]{2,1,0:T(8,128)} %param.8) | copy-start | bytes 98308
  0.7 16.1 %copy-start.24 = (bf16[1,64]{1,0:T(2,128)(2,1)S(1)}, bf16[1,64]{1,0:T(2,128)(2,1)}, u32[]{:S(2)}) copy-start(bf16[1,64]{1,0:T(2,128)(2,1)} %param.15) | copy-start | bytes 388
  1.4 10.8 %collective-permute-start = (f32[2,1,8,128]{3,2,1,0:T(8,128)S(1)}, f32[2,1,8,128]{3,2,1,0:T(8,128)S(1)}, u32[]{:S(2)}, u32[]{:S(2)}) collective-permute-start(f32[2,1,8,128]{3,2,1,0:T(8,128)S(1)} %get-tuple-element.44), channel_id=1, source_target_pairs={{0,4},{4,8},{8,12},{12,16},{16,20},{20,24},{24,28},{28,0},{1,5},{5... | collective-permute-start | bytes 24584 | tf_op jit(solution)/shard_map/ppermute | solution.py:16
  1.9 10.4 %collective-permute-start.1 = (f32[2,1,8,128]{3,2,1,0:T(8,128)S(1)}, f32[2,1,8,128]{3,2,1,0:T(8,128)S(1)}, u32[]{:S(2)}, u32[]{:S(2)}) collective-permute-start(f32[2,1,8,128]{3,2,1,0:T(8,128)S(1)} %get-tuple-element.45), channel_id=1, source_target_pairs={{4,0},{8,4},{12,8},{16,12},{20,16},{24,20},{28,24},{0,28},{5,1},{9... | collective-permute-start | bytes 24584 | tf_op jit(solution)/shard_map/ppermute | solution.py:18
  9.6 28.8 %copy-start.22 = (s32[128]{0:T(128)}, s32[128]{0:T(128)S(1)}, u32[]{:S(2)}) copy-start(s32[128]{0:T(128)S(1)} %fusion.31) | copy-start | bytes 1540
  10.2 9.9 %copy-start.20 = (f32[128]{0:T(128)}, f32[128]{0:T(128)S(1)}, u32[]{:S(2)}) copy-start(f32[128]{0:T(128)S(1)} %get-tuple-element.48) | copy-start | bytes 1540
  12.3 6.2 %collective-permute-start.2 = (f32[2,10,1,128]{3,2,1,0:T(1,128)S(1)}, f32[2,10,1,128]{3,2,1,0:T(1,128)S(1)}, u32[]{:S(2)}, u32[]{:S(2)}) collective-permute-start(f32[2,10,1,128]{3,2,1,0:T(1,128)S(1)} %get-tuple-element.42), channel_id=1, source_target_pairs={{0,1},{1,2},{2,3},{3,0},{4,5},{5,6},{6,7},{7,4},{8,9},{9,10},{10,1... | collective-permute-start | bytes 30728 | tf_op jit(solution)/shard_map/ppermute | solution.py:16
  14.7 3.8 %collective-permute-start.3 = (f32[2,10,1,128]{3,2,1,0:T(1,128)S(1)}, f32[2,10,1,128]{3,2,1,0:T(1,128)S(1)}, u32[]{:S(2)}, u32[]{:S(2)}) collective-permute-start(f32[2,10,1,128]{3,2,1,0:T(1,128)S(1)} %get-tuple-element.43), channel_id=1, source_target_pairs={{1,0},{2,1},{3,2},{0,3},{5,4},{6,5},{7,6},{4,7},{9,8},{10,9},{11,1... | collective-permute-start | bytes 30728 | tf_op jit(solution)/shard_map/ppermute | solution.py:18
  16.8 19.0 %copy-start.23 = (f32[64]{0:T(128)}, f32[64]{0:T(128)S(1)}, u32[]{:S(2)}) copy-start(f32[64]{0:T(128)S(1)} %bitcast_convert_fusion) | copy-start | bytes 772
  20.0 4.6 %copy-start.7 = (f32[8,8,127]{2,1,0:T(8,128)}, f32[8,8,127]{2,1,0:T(8,128)S(1)}, u32[]{:S(2)}) copy-start(f32[8,8,127]{2,1,0:T(8,128)S(1)} %get-tuple-element.35) | copy-start | bytes 97540
  20.0 4.6 %copy-start.9 = (f32[8,8,127]{2,1,0:T(8,128)}, f32[8,8,127]{2,1,0:T(8,128)S(1)}, u32[]{:S(2)}) copy-start(f32[8,8,127]{2,1,0:T(8,128)S(1)} %get-tuple-element.36) | copy-start | bytes 97540
  20.1 4.5 %copy-start.11 = (f32[8,8,1]{2,1,0:T(8,128)}, f32[8,8,1]{2,1,0:T(8,128)S(1)}, u32[]{:S(2)}) copy-start(f32[8,8,1]{2,1,0:T(8,128)S(1)} %get-tuple-element.33) | copy-start | bytes 772
  20.1 4.5 %copy-start.13 = (f32[8,8,1]{2,1,0:T(8,128)}, f32[8,8,1]{2,1,0:T(8,128)S(1)}, u32[]{:S(2)}) copy-start(f32[8,8,1]{2,1,0:T(8,128)S(1)} %get-tuple-element.34) | copy-start | bytes 772
  50.2 43.4 %copy-start.21 = (f32[128]{0:T(128)S(1)}, f32[128]{0:T(128)}, u32[]{:S(2)}) copy-start(f32[128]{0:T(128)} %copy-done.20) | copy-start | bytes 1540
  92.3 4.1 %copy-start.6 = (f32[8,8,128]{2,1,0:T(8,128)S(1)}, f32[8,8,128]{2,1,0:T(8,128)}, u32[]{:S(2)}) copy-start(f32[8,8,128]{2,1,0:T(8,128)} %param.8) | copy-start | bytes 98308
  92.3 4.1 %copy-start.8 = (f32[8,8,127]{2,1,0:T(8,128)S(1)}, f32[8,8,127]{2,1,0:T(8,128)}, u32[]{:S(2)}) copy-start(f32[8,8,127]{2,1,0:T(8,128)} %copy-done.7) | copy-start | bytes 97540
  92.3 4.1 %copy-start.10 = (f32[8,8,127]{2,1,0:T(8,128)S(1)}, f32[8,8,127]{2,1,0:T(8,128)}, u32[]{:S(2)}) copy-start(f32[8,8,127]{2,1,0:T(8,128)} %copy-done.9) | copy-start | bytes 97540
  92.3 4.1 %copy-start.12 = (f32[8,8,1]{2,1,0:T(8,128)S(1)}, f32[8,8,1]{2,1,0:T(8,128)}, u32[]{:S(2)}) copy-start(f32[8,8,1]{2,1,0:T(8,128)} %copy-done.11) | copy-start | bytes 772
  92.3 4.1 %copy-start.14 = (f32[8,8,1]{2,1,0:T(8,128)S(1)}, f32[8,8,1]{2,1,0:T(8,128)}, u32[]{:S(2)}) copy-start(f32[8,8,1]{2,1,0:T(8,128)} %copy-done.13) | copy-start | bytes 772
  93.6 3.5 %copy-start.1 = (f32[4,2,4,2,4,32,4]{5,3,1,6,4,2,0:T(2,128)S(1)}, f32[4,2,4,2,4,32,4]{5,3,1,6,4,2,0:T(2,128)}, u32[]{:S(2)}) copy-start(f32[4,2,4,2,4,32,4]{5,3,1,6,4,2,0:T(2,128)} %slice.246) | copy-start | bytes 393220
  100.1 15.1 %copy-start.4 = (f32[1,2,4,2,4,32,4]{5,3,1,6,4,2,0:T(2,128)S(1)}, f32[1,2,4,2,4,32,4]{5,3,1,6,4,2,0:T(2,128)}, u32[]{:S(2)}) copy-start(f32[1,2,4,2,4,32,4]{5,3,1,6,4,2,0:T(2,128)} %get-tuple-element.20) | copy-start | bytes 98308
  105.0 11.4 %copy-start.3 = (f32[1,2,4,2,4,32,4]{5,3,1,6,4,2,0:T(2,128)S(1)}, f32[1,2,4,2,4,32,4]{5,3,1,6,4,2,0:T(2,128)}, u32[]{:S(2)}) copy-start(f32[1,2,4,2,4,32,4]{5,3,1,6,4,2,0:T(2,128)} %get-tuple-element.21) | copy-start | bytes 98308
  105.0 4.1 %collective-permute-start.4 = (f32[4,1,8,128]{3,2,1,0:T(8,128)S(1)}, f32[4,1,8,128]{3,2,1,0:T(8,128)S(1)}, u32[]{:S(2)}, u32[]{:S(2)}) collective-permute-start(f32[4,1,8,128]{3,2,1,0:T(8,128)S(1)} %get-tuple-element.28), channel_id=1, source_target_pairs={{0,4},{4,8},{8,12},{12,16},{16,20},{20,24},{24,28},{28,0},{1,5},{5... | collective-permute-start | bytes 49160 | tf_op jit(solution)/shard_map/ppermute | solution.py:16
  105.1 4.1 %collective-permute-start.5 = (f32[4,1,8,128]{3,2,1,0:T(8,128)S(1)}, f32[4,1,8,128]{3,2,1,0:T(8,128)S(1)}, u32[]{:S(2)}, u32[]{:S(2)}) collective-permute-start(f32[4,1,8,128]{3,2,1,0:T(8,128)S(1)} %get-tuple-element.27), channel_id=1, source_target_pairs={{4,0},{8,4},{12,8},{16,12},{20,16},{24,20},{28,24},{0,28},{5,1},{9... | collective-permute-start | bytes 49160 | tf_op jit(solution)/shard_map/ppermute | solution.py:18
  109.2 9.5 %collective-permute-start.6 = (f32[4,10,1,128]{3,2,1,0:T(1,128)S(1)}, f32[4,10,1,128]{3,2,1,0:T(1,128)S(1)}, u32[]{:S(2)}, u32[]{:S(2)}) collective-permute-start(f32[4,10,1,128]{3,2,1,0:T(1,128)S(1)} %get-tuple-element.25), channel_id=1, source_target_pairs={{0,1},{1,2},{2,3},{3,0},{4,5},{5,6},{6,7},{7,4},{8,9},{9,10},{10,1... | collective-permute-start | bytes 61448 | tf_op jit(solution)/shard_map/ppermute | solution.py:16
  111.3 7.5 %collective-permute-start.7 = (f32[4,10,1,128]{3,2,1,0:T(1,128)S(1)}, f32[4,10,1,128]{3,2,1,0:T(1,128)S(1)}, u32[]{:S(2)}, u32[]{:S(2)}) collective-permute-start(f32[4,10,1,128]{3,2,1,0:T(1,128)S(1)} %get-tuple-element.26), channel_id=1, source_target_pairs={{1,0},{2,1},{3,2},{0,3},{5,4},{6,5},{7,6},{4,7},{9,8},{10,9},{11,1... | collective-permute-start | bytes 61448 | tf_op jit(solution)/shard_map/ppermute | solution.py:18
  116.5 2.3 %copy-start.15 = (f32[8,8,127]{2,1,0:T(8,128)S(1)}, f32[8,8,127]{2,1,0:T(8,128)}, u32[]{:S(2)}) copy-start(f32[8,8,127]{2,1,0:T(8,128)} %get-tuple-element.31) | copy-start | bytes 97540
  116.5 2.3 %copy-start.16 = (f32[8,8,127]{2,1,0:T(8,128)S(1)}, f32[8,8,127]{2,1,0:T(8,128)}, u32[]{:S(2)}) copy-start(f32[8,8,127]{2,1,0:T(8,128)} %get-tuple-element.32) | copy-start | bytes 97540
  116.5 2.3 %copy-start.17 = (f32[8,8,1]{2,1,0:T(8,128)S(1)}, f32[8,8,1]{2,1,0:T(8,128)}, u32[]{:S(2)}) copy-start(f32[8,8,1]{2,1,0:T(8,128)} %get-tuple-element.29) | copy-start | bytes 772
  116.5 2.3 %copy-start.18 = (f32[8,8,1]{2,1,0:T(8,128)S(1)}, f32[8,8,1]{2,1,0:T(8,128)}, u32[]{:S(2)}) copy-start(f32[8,8,1]{2,1,0:T(8,128)} %get-tuple-element.30) | copy-start | bytes 772
  (1 other events, 2.1 us)
where the time goes:
time: 121 us; the launch traced here: 120 us
  local copies, waits for them, and re-layouts  42.1 us (35%)
  blocking collectives  39.6 us (33%)
  starting transfers between devices  14.4 us (12%)
  other arithmetic  13.2 us (11%)
  matrix products  5.93 us (5%)
  waiting for transfers between devices  2.42 us (2%)
  between operations  1.96 us (2%)
    psum x1, blocking collectives, body(): total = lax.psum(flat, ('gx', 'gy'))  39.6 us
    another operation x15, local copies, waits for them, and re-layouts, closure_tile(): jnp.stack([center, padded[2:, 1:-1], padded[:-2, 1:-1], padded[1:-1, 2:],...  11.1 us
    ppermute x4, starting transfers between devices, padded_2(): lax.ppermute(head, axis, [((i + 1) % count, i) for i in range(count)])  9.39 us
    slice x3, local copies, waits for them, and re-layouts, closure_tile(): return (corr, local, dense[1:5], gin, gmid, gout)  8.91 us
    scatter-add x1, other arithmetic, closure_tile(): jnp.zeros((7, nblocks, 64), jnp.float32).at[:, ids]  5.09 us
    ppermute x4, starting transfers between devices, padded_2(): lax.ppermute(tail, axis, [(i, (i + 1) % count) for i in range(count)])  4.98 us
  transfers between devices with their start and end apart: 8, of which 2 were waited for; matrix products, arithmetic and copies ran while one was open for 11% of the time, Pallas kernels for 0%

commit v1 on v0

v1 whole, which is shorter than its diff:
```python
import functools

import jax
import jax.numpy as jnp
from jax import lax
from jax.experimental import pallas as pl
from jax.experimental.pallas import tpu as pltpu
from jax.sharding import PartitionSpec as P

viscosity = 0.1
MESH = pl.DeviceIdType.MESH
BF = jnp.bfloat16
F32 = jnp.float32


def iota(shape, dim):
    return lax.broadcasted_iota(jnp.int32, shape, dim)


def dot(a, b):
    return jnp.dot(a, b, preferred_element_type=F32)


def dot_nt(a, b):
    return lax.dot_general(a, b, (((1,), (1,)), ((), ())), preferred_element_type=F32)


def ones_where(mask):
    return jnp.where(mask, 1.0, 0.0).astype(BF)


def fluid_field(ids, count, fluid2):
    half, lanes = fluid2.shape
    cells = lanes // 2
    slots = ids.shape[1]
    lane = iota((1, slots), 1)
    live = jnp.where(lane < count, ids, -1).astype(F32)
    spread = jnp.broadcast_to(live, (half, slots))
    slot_of = iota((half, slots), 1)
    row = iota((half, slots), 0)
    fluid_t = jnp.transpose(fluid2.astype(F32)).astype(BF)
    block = iota((half, 512), 1) // 4
    placed = None
    for h in range(2):
        col = jnp.sum(jnp.where(slot_of == 2 * row + h, spread, 0.0), axis=1, keepdims=True)
        hot = ones_where(jnp.broadcast_to(col, (half, 512)) == block.astype(F32))
        part = dot(fluid_t[h * cells : (h + 1) * cells], hot)
        placed = part if placed is None else placed + part
    keep = (iota((cells, 512), 0) % 4) == (iota((cells, 512), 1) % 4)
    placed = jnp.where(keep, placed, 0.0).astype(BF)
    rhs = jnp.concatenate(
        [
            jnp.concatenate([placed[:, 0:128], placed[:, 256:384]], axis=1),
            jnp.concatenate([placed[:, 128:256], placed[:, 384:512]], axis=1),
        ],
        axis=0,
    )
    r = iota((32, 2 * cells), 0)
    c = iota((32, 2 * cells), 1)
    pick = (r // 8 == (c % 64) // 16) & ((r % 8) // 4 == c // 64) & (r % 4 == (c % 16) // 4)
    return dot(ones_where(pick), rhs)


def kernel(
    n, m, v_ref, c_ref, ids_ref, count_ref, fluid_ref, win_ref, wmid_ref, wout_ref,
    new_ref, grad_ref, tot_ref,
    hsend, hrecv, ssend, srecv, parts, rsbuf, gybuf, agbuf,
    hs_sem, hr_sem, ss_sem, sr_sem, rs_ssem, rs_rsem, gy_ssem, gy_rsem, ag_ssem, ag_rsem,
):
    px = lax.axis_index("gx")
    py = lax.axis_index("gy")
    rows = parts.shape[1]

    barrier = pltpu.get_barrier_semaphore()
    for d in range(1, n):
        pl.semaphore_signal(barrier, inc=1, device_id=(lax.rem(px + d, n), py), device_id_type=MESH)
    for d in range(1, m):
        pl.semaphore_signal(barrier, inc=1, device_id=(px, lax.rem(py + d, m)), device_id_type=MESH)

    v = v_ref[...]
    cot = c_ref[...]
    for f, field in enumerate((v, cot)):
        hsend[0, f] = field[0]
        hsend[1, f] = field[7]
        hsend[2, f] = field[:, 0, :]
        hsend[3, f] = field[:, 7, :]
    near = (
        (lax.rem(px + n - 1, n), py),
        (lax.rem(px + 1, n), py),
        (px, lax.rem(py + m - 1, m)),
        (px, lax.rem(py + 1, m)),
    )
    pl.semaphore_wait(barrier, n + m - 2)
    halo = [
        pltpu.make_async_remote_copy(
            src_ref=hsend.at[k], dst_ref=hrecv.at[k], send_sem=hs_sem.at[k], recv_sem=hr_sem.at[k],
            device_id=near[k], device_id_type=MESH,
        )
        for k in range(4)
    ]
    for copy in halo:
        copy.start()

    weight = fluid_field(ids_ref[...], count_ref[...], fluid_ref[...])
    win = win_ref[...]
    wmid = wmid_ref[...]
    wout = wout_ref[...]
    eye = ones_where(iota((64, 64), 0) == iota((64, 64), 1))
    wmid_t = dot_nt(eye, wmid).astype(BF)
    widen = ones_where(iota((7, 56), 0) == iota((7, 56), 1) // 8)
    win_y = dot(win, widen)
    tall = jnp.concatenate([win_y] * 8, axis=0)
    win_big = jnp.where(iota((512, 56), 0) // 64 == iota((512, 56), 1) % 8, tall, 0.0).astype(BF)
    repeat = ones_where(iota((64, 512), 0) == iota((64, 512), 1) % 64)
    widen_t = ones_where(iota((56, 7), 1) == iota((56, 7), 0) // 8)
    win_t = dot(dot_nt(widen_t, win).astype(BF), repeat)
    same_y = iota((56, 512), 0) % 8 == iota((56, 512), 1) // 64
    win_tbig = jnp.where(same_y, win_t, 0.0).astype(BF)
    wout_row = jnp.broadcast_to(dot(wout, repeat), (8, 512))
    wout_big = jnp.where(iota((8, 512), 0) == iota((8, 512), 1) // 64, wout_row, 0.0).astype(BF)
    wout_col = jnp.concatenate([dot_nt(eye, jnp.broadcast_to(wout, (8, 64)))] * 8, axis=0)
    wout_tbig = jnp.where(iota((512, 8), 0) // 64 == iota((512, 8), 1), wout_col, 0.0).astype(BF)

    row = iota((8, 128), 0)
    zup = [pltpu.roll(v[x], 127, 1) for x in range(8)]
    zdn = [pltpu.roll(v[x], 1, 1) for x in range(8)]

    for copy in halo:
        copy.wait()

    def beside(field, f, x):
        up = field[x + 1] if x < 7 else hrecv[0, f]
        down = field[x - 1] if x > 0 else hrecv[1, f]
        north = jnp.where(row == 7, hrecv[2, f, x : x + 1, :], pltpu.roll(field[x], 7, 0))
        south = jnp.where(row == 0, hrecv[3, f, x : x + 1, :], pltpu.roll(field[x], 1, 0))
        return [up, down, north, south]

    def cat_y(a):
        return jnp.concatenate([a[64 * y : 64 * y + 64] for y in range(8)], axis=1)

    def stack_y(a):
        return jnp.concatenate([a[:, 256 * y : 256 * y + 256] for y in range(8)], axis=0)

    gmid = jnp.zeros((64, 64), F32)
    gin = jnp.zeros((56, 512), F32)
    gout = jnp.zeros((8, 512), F32)
    dfs = []
    for pair in range(4):
        feats = []
        bases = []
        for x in (2 * pair, 2 * pair + 1):
            six = beside(v, 0, x) + [zup[x], zdn[x]]
            feats.append(jnp.concatenate([v[x]] + six, axis=0))
            bases.append(v[x] + viscosity * (sum(six[1:], six[0]) - 6.0 * v[x]))
        xin = jnp.concatenate(feats, axis=1).astype(BF)
        w = jnp.concatenate(
            [
                weight[8 * (x % 4) : 8 * (x % 4) + 8, 128 * (x // 4) : 128 * (x // 4) + 128]
                for x in (2 * pair, 2 * pair + 1)
            ],
            axis=1,
        )
        h1 = cat_y(jnp.tanh(dot(win_big, xin)).astype(BF))
        h2 = jnp.tanh(dot(wmid, h1)).astype(BF)
        h2s = stack_y(h2)
        corr = dot(wout_big, h2s) * w
        for i in range(2):
            new_ref[2 * pair + i] = bases[i] + corr[:, 128 * i : 128 * i + 128]
        dc = (jnp.concatenate([cot[2 * pair], cot[2 * pair + 1]], axis=1) * w).astype(BF)
        h2f = h2.astype(F32)
        h1f = h1.astype(F32)
        da2 = (cat_y(dot(wout_tbig, dc)) * (1.0 - h2f * h2f)).astype(BF)
        da1 = (dot(wmid_t, da2) * (1.0 - h1f * h1f)).astype(BF)
        da1s = stack_y(da1)
        df = dot(win_tbig, da1s)
        dfs += [df[:, :128], df[:, 128:]]
        gmid = gmid + dot_nt(da2, h1)
        gin = gin + dot_nt(xin, da1s)
        gout = gout + dot_nt(dc, h2s)

    both = jnp.concatenate([gin, gout], axis=0)
    both = jnp.where(iota((64, 512), 0) % 8 == iota((64, 512), 1) // 64, both, 0.0)
    both = jnp.sum(both.reshape(8, 8, 512), axis=1)
    both = both[:, 0:128] + both[:, 128:256] + both[:, 256:384] + both[:, 384:512]
    both = both + pltpu.roll(both, 64, 1)
    thin = jnp.concatenate([both[:, :64], jnp.zeros((56, 64), F32)], axis=0)
    parts[...] = jnp.concatenate([gmid, thin], axis=1).reshape(n, rows, 128)

    def send(src, dst, ssem, rsem, peer):
        copy = pltpu.make_async_remote_copy(
            src_ref=src, dst_ref=dst, send_sem=ssem, recv_sem=rsem, device_id=peer, device_id_type=MESH
        )
        return copy

    rs = []
    for d in range(1, n):
        peer = lax.rem(px + d, n)
        copy = send(parts.at[peer], rsbuf.at[d - 1], rs_ssem.at[d - 1], rs_rsem.at[d - 1], (peer, py))
        copy.start()
        rs.append(copy)

    ssend[0] = dfs[0][16:24]
    ssend[1] = dfs[7][8:16]
    for x in range(8):
        ssend[2, x : x + 1] = dfs[x][32:33]
        ssend[3, x : x + 1] = dfs[x][31:32]
    side = [
        pltpu.make_async_remote_copy(
            src_ref=ssend.at[k], dst_ref=srecv.at[k], send_sem=ss_sem.at[k], recv_sem=sr_sem.at[k],
            device_id=near[k], device_id_type=MESH,
        )
        for k in range(4)
    ]
    for copy in side:
        copy.start()

    for copy in rs:
        copy.wait()
    mine = parts[px]
    for d in range(n - 1):
        mine = mine + rsbuf[d]

    gybuf[py] = mine
    gy = []
    for d in range(1, m):
        peer = lax.rem(py + d, m)
        copy = send(gybuf.at[py], gybuf.at[py], gy_ssem.at[d - 1], gy_rsem.at[d - 1], (px, peer))
        copy.start()
        gy.append(copy)

    for copy in side:
        copy.wait()
    for x in range(8):
        six = beside(cot, 1, x) + [pltpu.roll(cot[x], 127, 1), pltpu.roll(cot[x], 1, 1)]
        out = cot[x] + viscosity * (sum(six[1:], six[0]) - 6.0 * cot[x])
        df = dfs[x]
        out = out + df[0:8] + pltpu.roll(df[40:48], 1, 1) + pltpu.roll(df[48:56], 127, 1)
        out = out + (dfs[x - 1][8:16] if x > 0 else srecv[1])
        out = out + (dfs[x + 1][16:24] if x < 7 else srecv[0])
        out = out + jnp.where(row == 0, srecv[3, x : x + 1, :], pltpu.roll(df[24:32], 1, 0))
        out = out + jnp.where(row == 7, srecv[2, x : x + 1, :], pltpu.roll(df[32:40], 7, 0))
        grad_ref[x] = out

    for copy in gy:
        copy.wait()
    total = gybuf[0]
    for d in range(1, m):
        total = total + gybuf[d]
    scale = 1.0 / jnp.sqrt(jnp.float32(n * m * ids_ref.shape[1] * 64))
    agbuf[px] = total * scale
    ag = []
    for d in range(1, n):
        copy = send(agbuf.at[px], agbuf.at[px], ag_ssem.at[d - 1], ag_rsem.at[d - 1], (lax.rem(px + d, n), py))
        copy.start()
        ag.append(copy)
    for copy in ag:
        copy.wait()
    tot_ref[...] = agbuf[...].reshape(n * rows, 128)


def body(n, m, velocity, cotangent, block_ids, fluid_count, fluid_cells, w_in, w_mid, w_out):
    slots = block_ids.shape[2]
    width = w_mid.shape[0]
    rows = -(-width // n)
    vmem = pl.BlockSpec(memory_space=pltpu.VMEM)
    dma = pltpu.SemaphoreType.DMA
    new_field, grad_field, total = pl.pallas_call(
        functools.partial(kernel, n, m),
        out_shape=(
            jax.ShapeDtypeStruct(velocity.shape, F32),
            jax.ShapeDtypeStruct(velocity.shape, F32),
            jax.ShapeDtypeStruct((n * rows, 128), F32),
        ),
        in_specs=[vmem] * 8,
        out_specs=(vmem, vmem, vmem),
        scratch_shapes=[
            pltpu.VMEM((4, 2, 8, 128), F32),
            pltpu.VMEM((4, 2, 8, 128), F32),
            pltpu.VMEM((4, 8, 128), F32),
            pltpu.VMEM((4, 8, 128), F32),
            pltpu.VMEM((n, rows, 128), F32),
            pltpu.VMEM((n - 1, rows, 128), F32),
            pltpu.VMEM((m, rows, 128), F32),
            pltpu.VMEM((n, rows, 128), F32),
            dma((4,)), dma((4,)), dma((4,)), dma((4,)),
            dma((n - 1,)), dma((n - 1,)), dma((m - 1,)), dma((m - 1,)), dma((n - 1,)), dma((n - 1,)),
        ],
        compiler_params=pltpu.CompilerParams(
            collective_id=0, has_side_effects=True, vmem_limit_bytes=48 * 1024 * 1024
        ),
    )(
        velocity,
        cotangent,
        block_ids.reshape(1, slots),
        fluid_count,
        fluid_cells.reshape(slots // 2, 128),
        w_in,
        w_mid,
        w_out,
    )
    return (
        new_field,
        grad_field,
        total[: w_in.shape[1], width : 2 * width].T,
        total[:width, :width],
        total[w_in.shape[1] : w_in.shape[1] + 1, width : 2 * width],
    )


def solution(mesh):
    n, m = mesh.shape["gx"], mesh.shape["gy"]
    in_specs = (
        P("gx", "gy", None),
        P("gx", "gy", None),
        P("gx", "gy", None),
        P("gx", "gy"),
        P("gx", "gy", None),
        P(),
        P(),
        P(),
    )
    out_specs = (P("gx", "gy", None), P("gx", "gy", None), P(), P(), P())
    return jax.shard_map(
        functools.partial(body, n, m), mesh=mesh, in_specs=in_specs, out_specs=out_specs, check_vma=False
    )
```

time: 121 us -> 30.2 us (0.25)
  blocking collectives: 39.6 us -> 0 us
  local copies, waits for them, and re-layouts: 42.1 us -> 6.17 us
  Pallas kernels: 0 us -> 22.3 us
  starting transfers between devices: 14.4 us -> 0 us
  other arithmetic: 13.2 us -> 0 us
  matrix products: 5.93 us -> 0 us
  waiting for transfers between devices: 2.42 us -> 0 us
    psum x1 -> x0, blocking collectives: 39.6 us -> none  [body(): total = lax.psum(flat, ('gx', 'gy'))]
    pallas_call x0 -> x1, Pallas kernels: none -> 22.3 us  [body(): pl.pallas_call(functools.partial(kernel, n, m), out_shape=(jax.ShapeDtype...]
    ppermute x8 -> x0, starting transfers between devices: 14.4 us -> none  [the longest x4 9.39 us: padded_2(): lax.ppermute(head, axis, [((i + 1) % count, i) for i in range(count)])]
    slice x19 -> x1, local copies, waits for them, and re-layouts: 13.6 us -> 0.58 us  [body(): total[w_in.shape[1]:w_in.shape[1] + 1, width:2 * width]]
    another operation x16 -> x0, local copies, waits for them, and re-layouts: 11.2 us -> none  [the longest x15 11.1 us: closure_tile(): jnp.stack([center, padded[2:, 1:-1], padded[:-2, 1:-1], padded[1:-1, 2:],...]
    reshape x14 -> x0, local copies, waits for them, and re-layouts: 6.95 us -> none  [the longest x1 1.83 us: to_blocks(): shaped = field.reshape(lead + (sizex // 4, 4, sizey // 4, 4, sizez // 4, 4))]
    scatter-add x2 -> x0, other arithmetic: 6.45 us -> none  [the longest x1 5.09 us: closure_tile(): jnp.zeros((7, nblocks, 64), jnp.float32).at[:, ids]]
    dot_general x7 -> x0, matrix products: 5.93 us -> none  [the longest x1 1.67 us: closure_tile(): lax.dot_general(dcl[None, :], h2, dims, preferred_element_type=jnp.float32)]
  transfers between devices with their start and end apart: 8 -> 0, of which waited for: 2 -> 0; matrix products, arithmetic and copies ran while one was open for 11% -> 0% of each run, Pallas kernels for 0% -> 0%
where the time goes in v1:
time: 30.2 us; the launch traced here: 29.9 us
  Pallas kernels  22.3 us (74%)
  local copies, waits for them, and re-layouts  6.17 us (20%)
  between operations  1.35 us (4%)
    pallas_call x1, Pallas kernels, body(): pl.pallas_call(functools.partial(kernel, n, m), out_shape=(jax.ShapeDtype...  22.3 us
    unnamed x16, local copies, waits for them, and re-layouts  4.92 us
    transpose x1, local copies, waits for them, and re-layouts, body(): total[:w_in.shape[1], width:2 * width]  0.66 us

profile of v1, /device:TPU:0, one launch (start us, length us, event | category | flops | bytes accessed | tf_op | source)
XLA Modules:
  0.0 29.9 jit_solution(10767011413594099927)
XLA Ops:
  0.6 0.0 copy-start.3
  1.3 0.0 copy-start.4
  1.3 0.0 copy-start.5
  1.3 0.8 %copy.13.win_ref = bf16[64,7]{1,0:T(8,128)(2,1)S(1)} copy(bf16[64,7]{0,1:T(8,128)(2,1)} %param.13) | data formatting | bytes 1792 | tf_op args[5]
  2.1 0.0 copy-done.3
  2.1 0.0 copy-done.4
  2.1 0.0 copy-done.5
  2.1 0.0 copy-start
  2.2 0.7 %copy-done = f32[8,8,128]{2,1,0:T(8,128)S(1)} copy-done((f32[8,8,128]{2,1,0:T(8,128)S(1)}, f32[8,8,128]{2,1,0:T(8,128)}, u32[]{:S(2)}) %copy-start) | copy-done | bytes 32792
  2.9 0.0 copy-start.1
  2.9 0.8 %copy-done.1 = f32[8,8,128]{2,1,0:T(8,128)S(1)} copy-done((f32[8,8,128]{2,1,0:T(8,128)S(1)}, f32[8,8,128]{2,1,0:T(8,128)}, u32[]{:S(2)}) %copy-start.1) | copy-done | bytes 32792
  3.7 0.0 copy-start.2
  3.7 0.8 %copy-done.2 = s32[1,1,8192]{2,1,0:T(1,128)S(1)} copy-done((s32[1,1,8192]{2,1,0:T(1,128)S(1)}, s32[1,1,8192]{2,1,0:T(1,128)}, u32[]{:S(2)}) %copy-start.2) | copy-done | bytes 32792
  4.4 22.3 %shard_map.119 = (f32[8,8,128]{2,1,0:T(8,128)S(1)}, f32[8,8,128]{2,1,0:T(8,128)S(1)}, f32[64,128]{1,0:T(8,128)S(1)}) custom-call(f32[8,8,128]{2,1,0:T(8,128)S(1)} %copy-done, f32[8,8,128]{2,1,0:T(8,128)S(1)} %copy-done.1, s32[1,128]{1,0:T(1,128)S(1)} %bitcast.7, s32[1,1]{1,0:T(1,128)S(6)} %copy.17.count_ref, s32[64,128]{1,0:T(8,128)S(1)} %bitcast.6, ...), custom_call_target="tpu_custom_call" | custom-call | tf_op jit(solution)/shard_map/pallas_call | solution.py:267
  26.8 0.6 %slice.11 = f32[1,64]{1,0:T(1,128)} slice(f32[64,128]{1,0:T(8,128)S(1)} %get-tuple-element.10), slice={[7:8], [64:128]} | slice | bytes 512 | tf_op jit(solution)/shard_map/slice | solution.py:306
  27.3 0.7 %slice_bitcast_fusion = f32[64,7]{0,1:T(8,128)} fusion(f32[64,128]{1,0:T(8,128)S(1)} %get-tuple-element.10), kind=kLoop, calls=%fused_computation | loop fusion | bytes 3584 | tf_op jit(solution)/shard_map/transpose | solution.py:304
  28.0 0.6 %copy.18 = f32[8,8,128]{2,1,0:T(8,128)} copy(f32[8,8,128]{2,1,0:T(8,128)S(1)} %get-tuple-element.16) | data formatting | bytes 65536
  28.6 0.6 %copy.19 = f32[8,8,128]{2,1,0:T(8,128)} copy(f32[8,8,128]{2,1,0:T(8,128)S(1)} %get-tuple-element.17) | data formatting | bytes 65536
  29.2 0.6 %copy.20 = f32[64,64]{1,0:T(8,128)} copy(f32[64,64]{1,0:T(8,128)S(1)} %bitcast.5) | data formatting | bytes 32768
Async XLA Ops:
  0.6 1.5 %copy-start.3 = (bf16[64,64]{1,0:T(8,128)(2,1)S(1)}, bf16[64,64]{1,0:T(8,128)(2,1)}, u32[]{:S(2)}) copy-start(bf16[64,64]{1,0:T(8,128)(2,1)} %wmid_ref.1) | copy-start | bytes 24580
  1.3 0.8 %copy-start.4 = (s32[1,1,128]{2,1,0:T(1,128)S(1)}, s32[1,1,128]{2,1,0:T(1,128)}, u32[]{:S(2)}) copy-start(s32[1,1,128]{2,1,0:T(1,128)} %param.10) | copy-start | bytes 1540
  1.3 0.8 %copy-start.5 = (bf16[1,64]{1,0:T(2,128)(2,1)S(1)}, bf16[1,64]{1,0:T(2,128)(2,1)}, u32[]{:S(2)}) copy-start(bf16[1,64]{1,0:T(2,128)(2,1)} %wout_ref.1) | copy-start | bytes 388
  2.1 0.8 %copy-start = (f32[8,8,128]{2,1,0:T(8,128)S(1)}, f32[8,8,128]{2,1,0:T(8,128)}, u32[]{:S(2)}) copy-start(f32[8,8,128]{2,1,0:T(8,128)} %v_ref.1) | copy-start | bytes 98308
  2.9 0.8 %copy-start.1 = (f32[8,8,128]{2,1,0:T(8,128)S(1)}, f32[8,8,128]{2,1,0:T(8,128)}, u32[]{:S(2)}) copy-start(f32[8,8,128]{2,1,0:T(8,128)} %c_ref.1) | copy-start | bytes 98308
  3.7 0.8 %copy-start.2 = (s32[1,1,8192]{2,1,0:T(1,128)S(1)}, s32[1,1,8192]{2,1,0:T(1,128)}, u32[]{:S(2)}) copy-start(s32[1,1,8192]{2,1,0:T(1,128)} %param.12) | copy-start | bytes 98308

commit v2 on v1

--- a/solution.py
+++ b/solution.py
@@ -62,8 +62,10 @@
 
 
 def kernel(
-    n, m, v_ref, c_ref, ids_ref, count_ref, fluid_ref, win_ref, wmid_ref, wout_ref,
-    new_ref, grad_ref, tot_ref,
+    n, m, v_hbm, c_hbm, ids_hbm, count_ref, fluid_hbm, win_hbm, wmid_hbm, wout_hbm,
+    new_hbm, grad_hbm, gin_hbm, gmid_hbm, gout_hbm,
+    new_ref, grad_ref, gin_ref, gmid_ref, gout_ref, out_sem,
+    v_ref, c_ref, ids_ref, fluid_ref, win_ref, wmid_ref, wout_ref, in_sem,
     hsend, hrecv, ssend, srecv, parts, rsbuf, gybuf, agbuf,
     hs_sem, hr_sem, ss_sem, sr_sem, rs_ssem, rs_rsem, gy_ssem, gy_rsem, ag_ssem, ag_rsem,
 ):
@@ -71,12 +73,31 @@
     py = lax.axis_index("gy")
     rows = parts.shape[1]
 
+    loads = [
+        pltpu.make_async_copy(src, dst, in_sem.at[k])
+        for k, (src, dst) in enumerate(
+            (
+                (v_hbm, v_ref),
+                (c_hbm, c_ref),
+                (ids_hbm, ids_ref),
+                (fluid_hbm, fluid_ref),
+                (win_hbm, win_ref),
+                (wmid_hbm, wmid_ref),
+                (wout_hbm, wout_ref),
+            )
+        )
+    ]
+    for load in loads:
+        load.start()
+
     barrier = pltpu.get_barrier_semaphore()
     for d in range(1, n):
         pl.semaphore_signal(barrier, inc=1, device_id=(lax.rem(px + d, n), py), device_id_type=MESH)
     for d in range(1, m):
         pl.semaphore_signal(barrier, inc=1, device_id=(px, lax.rem(py + d, m)), device_id_type=MESH)
 
+    loads[0].wait()
+    loads[1].wait()
     v = v_ref[...]
     cot = c_ref[...]
     for f, field in enumerate((v, cot)):
@@ -101,6 +122,8 @@
     for copy in halo:
         copy.start()
 
+    for load in loads[2:]:
+        load.wait()
     weight = fluid_field(ids_ref[...], count_ref[...], fluid_ref[...])
     win = win_ref[...]
     wmid = wmid_ref[...]
@@ -108,12 +131,12 @@
     eye = ones_where(iota((64, 64), 0) == iota((64, 64), 1))
     wmid_t = dot_nt(eye, wmid).astype(BF)
     widen = ones_where(iota((7, 56), 0) == iota((7, 56), 1) // 8)
-    win_y = dot(win, widen)
+    win_y = dot(dot_nt(eye, win).astype(BF), widen)
     tall = jnp.concatenate([win_y] * 8, axis=0)
     win_big = jnp.where(iota((512, 56), 0) // 64 == iota((512, 56), 1) % 8, tall, 0.0).astype(BF)
     repeat = ones_where(iota((64, 512), 0) == iota((64, 512), 1) % 64)
     widen_t = ones_where(iota((56, 7), 1) == iota((56, 7), 0) // 8)
-    win_t = dot(dot_nt(widen_t, win).astype(BF), repeat)
+    win_t = dot(dot(widen_t, win).astype(BF), repeat)
     same_y = iota((56, 512), 0) % 8 == iota((56, 512), 1) // 64
     win_tbig = jnp.where(same_y, win_t, 0.0).astype(BF)
     wout_row = jnp.broadcast_to(dot(wout, repeat), (8, 512))
@@ -228,6 +251,9 @@
         copy.start()
         gy.append(copy)
 
+    new_out = pltpu.make_async_copy(new_ref, new_hbm, out_sem.at[0])
+    new_out.start()
+
     for copy in side:
         copy.wait()
     for x in range(8):
@@ -240,6 +266,8 @@
         out = out + jnp.where(row == 0, srecv[3, x : x + 1, :], pltpu.roll(df[24:32], 1, 0))
         out = out + jnp.where(row == 7, srecv[2, x : x + 1, :], pltpu.roll(df[32:40], 7, 0))
         grad_ref[x] = out
+    grad_out = pltpu.make_async_copy(grad_ref, grad_hbm, out_sem.at[1])
+    grad_out.start()
 
     for copy in gy:
         copy.wait()
@@ -255,7 +283,30 @@
         ag.append(copy)
     for copy in ag:
         copy.wait()
-    tot_ref[...] = agbuf[...].reshape(n * rows, 128)
+    total = agbuf[...].reshape(n * rows, 128)
+    gmid_ref[...] = total[:64, :64]
+    last = pltpu.roll(total[:8], 64, 1)[:, :64]
+    gin_ref[...] = last[:7]
+    gout_ref[...] = last[7:8]
+    outs = [
+        pltpu.make_async_copy(gin_ref, gin_hbm, out_sem.at[2]),
+        pltpu.make_async_copy(gmid_ref, gmid_hbm, out_sem.at[3]),
+        pltpu.make_async_copy(gout_ref, gout_hbm, out_sem.at[4]),
+    ]
+    for copy in outs:
+        copy.start()
+    for copy in [new_out, grad_out] + outs:
+        copy.wait()
+
+
+def hand_on(*refs):
+    sem = refs[-1]
+    half = len(refs) // 2
+    copies = [pltpu.make_async_copy(refs[k], refs[half + k], sem.at[k]) for k in range(half)]
+    for copy in copies:
+        copy.start()
+    for copy in copies:
+        copy.wait()
 
 
 def body(n, m, velocity, cotangent, block_ids, fluid_count, fluid_cells, w_in, w_mid, w_out):
@@ -263,17 +314,31 @@
     width = w_mid.shape[0]
     rows = -(-width // n)
     vmem = pl.BlockSpec(memory_space=pltpu.VMEM)
+    hbm = pl.BlockSpec(memory_space=pltpu.HBM)
     dma = pltpu.SemaphoreType.DMA
-    new_field, grad_field, total = pl.pallas_call(
+    outs = (
+        jax.ShapeDtypeStruct(velocity.shape, F32),
+        jax.ShapeDtypeStruct(velocity.shape, F32),
+        jax.ShapeDtypeStruct(w_in.shape[::-1], F32),
+        jax.ShapeDtypeStruct(w_mid.shape, F32),
+        jax.ShapeDtypeStruct(w_out.shape, F32),
+    )
+    results = pl.pallas_call(
         functools.partial(kernel, n, m),
-        out_shape=(
-            jax.ShapeDtypeStruct(velocity.shape, F32),
-            jax.ShapeDtypeStruct(velocity.shape, F32),
-            jax.ShapeDtypeStruct((n * rows, 128), F32),
-        ),
-        in_specs=[vmem] * 8,
-        out_specs=(vmem, vmem, vmem),
-        scratch_shapes=[
+        out_shape=outs,
+        in_specs=[hbm] * 3 + [vmem] + [hbm] * 4,
+        out_specs=(hbm,) * 5,
+        scratch_shapes=[pltpu.VMEM(out.shape, F32) for out in outs]
+        + [
+            dma((5,)),
+            pltpu.VMEM(velocity.shape, F32),
+            pltpu.VMEM(velocity.shape, F32),
+            pltpu.VMEM((1, slots), jnp.int32),
+            pltpu.VMEM((slots // 2, 128), jnp.int32),
+            pltpu.VMEM(w_in.shape[::-1], BF),
+            pltpu.VMEM(w_mid.shape, BF),
+            pltpu.VMEM(w_out.shape, BF),
+            dma((7,)),
             pltpu.VMEM((4, 2, 8, 128), F32),
             pltpu.VMEM((4, 2, 8, 128), F32),
             pltpu.VMEM((4, 8, 128), F32),
@@ -286,7 +351,7 @@
             dma((n - 1,)), dma((n - 1,)), dma((m - 1,)), dma((m - 1,)), dma((n - 1,)), dma((n - 1,)),
         ],
         compiler_params=pltpu.CompilerParams(
-            collective_id=0, has_side_effects=True, vmem_limit_bytes=48 * 1024 * 1024
+            collective_id=0, has_side_effects=True, vmem_limit_bytes=65300 * 1024
         ),
     )(
         velocity,
@@ -294,17 +359,19 @@
         block_ids.reshape(1, slots),
         fluid_count,
         fluid_cells.reshape(slots // 2, 128),
-        w_in,
+        w_in.T,
         w_mid,
         w_out,
     )
-    return (
-        new_field,
-        grad_field,
-        total[: w_in.shape[1], width : 2 * width].T,
-        total[:width, :width],
-        total[w_in.shape[1] : w_in.shape[1] + 1, width : 2 * width],
-    )
+    new_field, grad_field, gin_t, gmid, gout = pl.pallas_call(
+        hand_on,
+        out_shape=outs,
+        in_specs=[hbm] * 5,
+        out_specs=(hbm,) * 5,
+        scratch_shapes=[dma((5,))],
+        compiler_params=pltpu.CompilerParams(vmem_limit_bytes=65300 * 1024),
+    )(*results)
+    return new_field, grad_field, gin_t.T, gmid, gout
 
 
 def solution(mesh):

time: 30.2 us -> 29 us (0.960)
  local copies, waits for them, and re-layouts: 6.17 us -> 0 us
  Pallas kernels: 22.3 us -> 27.5 us
    pallas_call x1 -> x2, Pallas kernels: 22.3 us -> 27.5 us  [the longest x1 23.2 us: body(): pl.pallas_call(functools.partial(kernel, n, m), out_shape=outs, in_specs=...]
    unnamed x16 -> x0, local copies, waits for them, and re-layouts: 4.92 us -> none
    transpose x1 -> x0, local copies, waits for them, and re-layouts: 0.66 us -> none  [body(): total[:w_in.shape[1], width:2 * width]]
    slice x1 -> x0, local copies, waits for them, and re-layouts: 0.58 us -> none  [body(): total[w_in.shape[1]:w_in.shape[1] + 1, width:2 * width]]
where the time goes in v2:
time: 29 us; the launch traced here: 28.8 us
  Pallas kernels  27.5 us (95%)
  between operations  1.29 us (4%)
    pallas_call x1, Pallas kernels, body(): pl.pallas_call(functools.partial(kernel, n, m), out_shape=outs, in_specs=...  23.2 us
    pallas_call x1, Pallas kernels, body(): pl.pallas_call(hand_on, out_shape=outs, in_specs=[hbm] * 5, out_specs=(hb...  4.25 us

profile of v2, /device:TPU:0, one launch (start us, length us, event | category | flops | bytes accessed | tf_op | source)
XLA Modules:
  0.0 28.8 jit_solution(17093298858436993184)
XLA Ops:
  1.3 23.2 %shard_map.119 = (f32[8,8,128]{2,1,0:T(8,128)}, f32[8,8,128]{2,1,0:T(8,128)}, f32[7,64]{1,0:T(8,128)}, f32[64,64]{1,0:T(8,128)}, f32[1,64]{1,0:T(1,128)}) custom-call(f32[8,8,128]{2,1,0:T(8,128)} %v_hbm.1, f32[8,8,128]{2,1,0:T(8,128)} %c_hbm.1, s32[1,128]{1,0:T(1,128)} %bitcast.6, s32[1,1]{1,0:T(1,128)S(6)} %copy.13.count_ref, s32[64,128]{1,0:T(8,128)} %bitcast.4, ...), custom_call_target="tpu_custom_call" | custom-call | tf_op jit(solution)/shard_map/pallas_call | solution.py:326
  24.5 4.3 %shard_map.120 = (f32[8,8,128]{2,1,0:T(8,128)}, f32[8,8,128]{2,1,0:T(8,128)}, f32[7,64]{1,0:T(8,128)}, f32[64,64]{1,0:T(8,128)}, f32[1,64]{1,0:T(1,128)}) custom-call(f32[8,8,128]{2,1,0:T(8,128)} %get-tuple-element.15.refs_0_, f32[8,8,128]{2,1,0:T(8,128)} %get-tuple-element.16.refs_1_, f32[7,64]{1,0:T(8,128)} %get-tuple-element.17.refs_2_, ...), custom_call_target="tpu_custom_call" | custom-call | tf_op jit(solution)/shard_map/pallas_call | solution.py:366

commit v3 on v2

--- a/solution.py
+++ b/solution.py
@@ -66,12 +66,11 @@
     new_hbm, grad_hbm, gin_hbm, gmid_hbm, gout_hbm,
     new_ref, grad_ref, gin_ref, gmid_ref, gout_ref, out_sem,
     v_ref, c_ref, ids_ref, fluid_ref, win_ref, wmid_ref, wout_ref, in_sem,
-    hsend, hrecv, ssend, srecv, parts, rsbuf, gybuf, agbuf,
-    hs_sem, hr_sem, ss_sem, sr_sem, rs_ssem, rs_rsem, gy_ssem, gy_rsem, ag_ssem, ag_rsem,
+    hsend, hrecv, ssend, srecv, gybuf, agbuf,
+    hs_sem, hr_sem, ss_sem, sr_sem, gy_ssem, gy_rsem, ag_ssem, ag_rsem,
 ):
     px = lax.axis_index("gx")
     py = lax.axis_index("gy")
-    rows = parts.shape[1]
 
     loads = [
         pltpu.make_async_copy(src, dst, in_sem.at[k])
@@ -114,10 +113,11 @@
     pl.semaphore_wait(barrier, n + m - 2)
     halo = [
         pltpu.make_async_remote_copy(
-            src_ref=hsend.at[k], dst_ref=hrecv.at[k], send_sem=hs_sem.at[k], recv_sem=hr_sem.at[k],
+            src_ref=hsend.at[k, f], dst_ref=hrecv.at[k, f], send_sem=hs_sem.at[k, f], recv_sem=hr_sem.at[k, f],
             device_id=near[k], device_id_type=MESH,
         )
-        for k in range(4)
+        for f in range(2)
+        for k in (3, 2, 1, 0)
     ]
     for copy in halo:
         copy.start()
@@ -148,7 +148,7 @@
     zup = [pltpu.roll(v[x], 127, 1) for x in range(8)]
     zdn = [pltpu.roll(v[x], 1, 1) for x in range(8)]
 
-    for copy in halo:
+    for copy in halo[:4]:
         copy.wait()
 
     def beside(field, f, x):
@@ -206,8 +206,8 @@
     both = jnp.sum(both.reshape(8, 8, 512), axis=1)
     both = both[:, 0:128] + both[:, 128:256] + both[:, 256:384] + both[:, 384:512]
     both = both + pltpu.roll(both, 64, 1)
-    thin = jnp.concatenate([both[:, :64], jnp.zeros((56, 64), F32)], axis=0)
-    parts[...] = jnp.concatenate([gmid, thin], axis=1).reshape(n, rows, 128)
+    packed = jnp.concatenate([jnp.concatenate([gmid[:32], gmid[32:]], axis=1), both[:, :128]], axis=0)
+    gybuf[py] = packed
 
     def send(src, dst, ssem, rsem, peer):
         copy = pltpu.make_async_remote_copy(
@@ -215,12 +215,12 @@
         )
         return copy
 
-    rs = []
-    for d in range(1, n):
-        peer = lax.rem(px + d, n)
-        copy = send(parts.at[peer], rsbuf.at[d - 1], rs_ssem.at[d - 1], rs_rsem.at[d - 1], (peer, py))
-        copy.start()
-        rs.append(copy)
+    gy = []
+    for d in range(1, m):
+        peer = lax.rem(py + d, m)
+        copy = send(gybuf.at[py], gybuf.at[py], gy_ssem.at[d - 1], gy_rsem.at[d - 1], (px, peer))
+        copy.start()
+        gy.append(copy)
 
     ssend[0] = dfs[0][16:24]
     ssend[1] = dfs[7][8:16]
@@ -237,24 +237,22 @@
     for copy in side:
         copy.start()
 
-    for copy in rs:
-        copy.wait()
-    mine = parts[px]
-    for d in range(n - 1):
-        mine = mine + rsbuf[d]
-
-    gybuf[py] = mine
-    gy = []
+    for copy in gy:
+        copy.wait()
+    total = gybuf[0]
     for d in range(1, m):
-        peer = lax.rem(py + d, m)
-        copy = send(gybuf.at[py], gybuf.at[py], gy_ssem.at[d - 1], gy_rsem.at[d - 1], (px, peer))
-        copy.start()
-        gy.append(copy)
+        total = total + gybuf[d]
+    agbuf[px] = total
+    ag = []
+    for d in range(1, n):
+        copy = send(agbuf.at[px], agbuf.at[px], ag_ssem.at[d - 1], ag_rsem.at[d - 1], (lax.rem(px + d, n), py))
+        copy.start()
+        ag.append(copy)
 
     new_out = pltpu.make_async_copy(new_ref, new_hbm, out_sem.at[0])
     new_out.start()
 
-    for copy in side:
+    for copy in halo[4:] + side:
         copy.wait()
     for x in range(8):
         six = beside(cot, 1, x) + [pltpu.roll(cot[x], 127, 1), pltpu.roll(cot[x], 1, 1)]
@@ -269,23 +267,14 @@
     grad_out = pltpu.make_async_copy(grad_ref, grad_hbm, out_sem.at[1])
     grad_out.start()
 
-    for copy in gy:
-        copy.wait()
-    total = gybuf[0]
-    for d in range(1, m):
-        total = total + gybuf[d]
-    scale = 1.0 / jnp.sqrt(jnp.float32(n * m * ids_ref.shape[1] * 64))
-    agbuf[px] = total * scale
-    ag = []
+    for copy in ag:
+        copy.wait()
+    total = agbuf[0]
     for d in range(1, n):
-        copy = send(agbuf.at[px], agbuf.at[px], ag_ssem.at[d - 1], ag_rsem.at[d - 1], (lax.rem(px + d, n), py))
-        copy.start()
-        ag.append(copy)
-    for copy in ag:
-        copy.wait()
-    total = agbuf[...].reshape(n * rows, 128)
-    gmid_ref[...] = total[:64, :64]
-    last = pltpu.roll(total[:8], 64, 1)[:, :64]
+        total = total + agbuf[d]
+    total = total * (1.0 / jnp.sqrt(jnp.float32(n * m * ids_ref.shape[1] * 64)))
+    gmid_ref[...] = jnp.concatenate([total[:32, :64], pltpu.roll(total[:32], 64, 1)[:, :64]], axis=0)
+    last = total[32:40, :64]
     gin_ref[...] = last[:7]
     gout_ref[...] = last[7:8]
     outs = [
@@ -300,19 +289,21 @@
 
 
 def hand_on(*refs):
-    sem = refs[-1]
-    half = len(refs) // 2
-    copies = [pltpu.make_async_copy(refs[k], refs[half + k], sem.at[k]) for k in range(half)]
-    for copy in copies:
-        copy.start()
-    for copy in copies:
+    ins, outs, bufs, isem, osem = refs[:5], refs[5:10], refs[10:15], refs[15], refs[16]
+    a = [pltpu.make_async_copy(ins[k], bufs[k], isem.at[k]) for k in range(5)]
+    b = [pltpu.make_async_copy(bufs[k], outs[k], osem.at[k]) for k in range(5)]
+    for copy in a:
+        copy.start()
+    for k in range(5):
+        a[k].wait()
+        b[k].start()
+    for copy in b:
         copy.wait()
 
 
 def body(n, m, velocity, cotangent, block_ids, fluid_count, fluid_cells, w_in, w_mid, w_out):
     slots = block_ids.shape[2]
     width = w_mid.shape[0]
-    rows = -(-width // n)
     vmem = pl.BlockSpec(memory_space=pltpu.VMEM)
     hbm = pl.BlockSpec(memory_space=pltpu.HBM)
     dma = pltpu.SemaphoreType.DMA
@@ -343,12 +334,10 @@
             pltpu.VMEM((4, 2, 8, 128), F32),
             pltpu.VMEM((4, 8, 128), F32),
             pltpu.VMEM((4, 8, 128), F32),
-            pltpu.VMEM((n, rows, 128), F32),
-            pltpu.VMEM((n - 1, rows, 128), F32),
-            pltpu.VMEM((m, rows, 128), F32),
-            pltpu.VMEM((n, rows, 128), F32),
-            dma((4,)), dma((4,)), dma((4,)), dma((4,)),
-            dma((n - 1,)), dma((n - 1,)), dma((m - 1,)), dma((m - 1,)), dma((n - 1,)), dma((n - 1,)),
+            pltpu.VMEM((m, width // 2 + 8, 128), F32),
+            pltpu.VMEM((n, width // 2 + 8, 128), F32),
+            dma((4, 2)), dma((4, 2)), dma((4,)), dma((4,)),
+            dma((m - 1,)), dma((m - 1,)), dma((n - 1,)), dma((n - 1,)),
         ],
         compiler_params=pltpu.CompilerParams(
             collective_id=0, has_side_effects=True, vmem_limit_bytes=65300 * 1024
@@ -368,7 +357,7 @@
         out_shape=outs,
         in_specs=[hbm] * 5,
         out_specs=(hbm,) * 5,
-        scratch_shapes=[dma((5,))],
+        scratch_shapes=[pltpu.VMEM(out.shape, F32) for out in outs] + [dma((5,)), dma((5,))],
         compiler_params=pltpu.CompilerParams(vmem_limit_bytes=65300 * 1024),
     )(*results)
     return new_field, grad_field, gin_t.T, gmid, gout

time: 29 us -> 24.2 us (0.83)
  Pallas kernels: 27.5 us -> 22.6 us
    pallas_call x1, Pallas kernels: 4.25 us -> 1.5 us  [body(): pl.pallas_call(hand_on, out_shape=outs, in_specs=[hbm] * 5, out_specs=(hb...]
    pallas_call x1, Pallas kernels: 23.2 us -> 21.1 us  [body(): pl.pallas_call(functools.partial(kernel, n, m), out_shape=outs, in_specs=...]
where the time goes in v3:
time: 24.2 us; the launch traced here: 23.9 us
  Pallas kernels  22.6 us (93%)
  between operations  1.29 us (5%)
    pallas_call x1, Pallas kernels, body(): pl.pallas_call(functools.partial(kernel, n, m), out_shape=outs, in_specs=...  21.1 us
    pallas_call x1, Pallas kernels, body(): pl.pallas_call(hand_on, out_shape=outs, in_specs=[hbm] * 5, out_specs=(hb...  1.5 us

profile of v3, /device:TPU:0, one launch (start us, length us, event | category | flops | bytes accessed | tf_op | source)
XLA Modules:
  0.0 23.9 jit_solution(14197018538887632229)
XLA Ops:
  1.3 21.1 %shard_map.119 = (f32[8,8,128]{2,1,0:T(8,128)}, f32[8,8,128]{2,1,0:T(8,128)}, f32[7,64]{1,0:T(8,128)}, f32[64,64]{1,0:T(8,128)}, f32[1,64]{1,0:T(1,128)}) custom-call(f32[8,8,128]{2,1,0:T(8,128)} %v_hbm.1, f32[8,8,128]{2,1,0:T(8,128)} %c_hbm.1, s32[1,128]{1,0:T(1,128)} %bitcast.6, s32[1,1]{1,0:T(1,128)S(6)} %copy.13.count_ref, s32[64,128]{1,0:T(8,128)} %bitcast.4, ...), custom_call_target="tpu_custom_call" | custom-call | tf_op jit(solution)/shard_map/pallas_call | solution.py:317
  22.4 1.5 %shard_map.120 = (f32[8,8,128]{2,1,0:T(8,128)}, f32[8,8,128]{2,1,0:T(8,128)}, f32[7,64]{1,0:T(8,128)}, f32[64,64]{1,0:T(8,128)}, f32[1,64]{1,0:T(1,128)}) custom-call(f32[8,8,128]{2,1,0:T(8,128)} %get-tuple-element.15.refs_0_, f32[8,8,128]{2,1,0:T(8,128)} %get-tuple-element.16.refs_1_, f32[7,64]{1,0:T(8,128)} %get-tuple-element.17.refs_2_, ...), custom_call_target="tpu_custom_call" | custom-call | tf_op jit(solution)/shard_map/pallas_call | solution.py:355

commit v4 on v3

--- a/solution.py
+++ b/solution.py
@@ -167,7 +167,7 @@
     gmid = jnp.zeros((64, 64), F32)
     gin = jnp.zeros((56, 512), F32)
     gout = jnp.zeros((8, 512), F32)
-    dfs = []
+    later = []
     for pair in range(4):
         feats = []
         bases = []
@@ -186,17 +186,13 @@
         h1 = cat_y(jnp.tanh(dot(win_big, xin)).astype(BF))
         h2 = jnp.tanh(dot(wmid, h1)).astype(BF)
         h2s = stack_y(h2)
-        corr = dot(wout_big, h2s) * w
-        for i in range(2):
-            new_ref[2 * pair + i] = bases[i] + corr[:, 128 * i : 128 * i + 128]
         dc = (jnp.concatenate([cot[2 * pair], cot[2 * pair + 1]], axis=1) * w).astype(BF)
         h2f = h2.astype(F32)
         h1f = h1.astype(F32)
         da2 = (cat_y(dot(wout_tbig, dc)) * (1.0 - h2f * h2f)).astype(BF)
         da1 = (dot(wmid_t, da2) * (1.0 - h1f * h1f)).astype(BF)
         da1s = stack_y(da1)
-        df = dot(win_tbig, da1s)
-        dfs += [df[:, :128], df[:, 128:]]
+        later.append((bases, h2s, w, da1s))
         gmid = gmid + dot_nt(da2, h1)
         gin = gin + dot_nt(xin, da1s)
         gout = gout + dot_nt(dc, h2s)
@@ -222,6 +218,10 @@
         copy.start()
         gy.append(copy)
 
+    dfs = []
+    for _, _, _, da1s in later:
+        df = dot(win_tbig, da1s)
+        dfs += [df[:, :128], df[:, 128:]]
     ssend[0] = dfs[0][16:24]
     ssend[1] = dfs[7][8:16]
     for x in range(8):
@@ -236,6 +236,11 @@
     ]
     for copy in side:
         copy.start()
+
+    for pair, (bases, h2s, w, _) in enumerate(later):
+        corr = dot(wout_big, h2s) * w
+        for i in range(2):
+            new_ref[2 * pair + i] = bases[i] + corr[:, 128 * i : 128 * i + 128]
 
     for copy in gy:
         copy.wait()

time: 24.2 us -> 23.1 us (0.955)
  Pallas kernels: 22.6 us -> 21.6 us
    pallas_call x1, Pallas kernels: 21.1 us -> 20.1 us  [body(): pl.pallas_call(functools.partial(kernel, n, m), out_shape=outs, in_specs=...]
where the time goes in v4:
time: 23.1 us; the launch traced here: 22.9 us
  Pallas kernels  21.6 us (94%)
  between operations  1.29 us (6%)
    pallas_call x1, Pallas kernels, body(): pl.pallas_call(functools.partial(kernel, n, m), out_shape=outs, in_specs=...  20.1 us
    pallas_call x1, Pallas kernels, body(): pl.pallas_call(hand_on, out_shape=outs, in_specs=[hbm] * 5, out_specs=(hb...  1.5 us

profile of v4, /device:TPU:0, one launch (start us, length us, event | category | flops | bytes accessed | tf_op | source)
XLA Modules:
  0.0 22.9 jit_solution(9560583034202175439)
XLA Ops:
  1.3 20.1 %shard_map.119 = (f32[8,8,128]{2,1,0:T(8,128)}, f32[8,8,128]{2,1,0:T(8,128)}, f32[7,64]{1,0:T(8,128)}, f32[64,64]{1,0:T(8,128)}, f32[1,64]{1,0:T(1,128)}) custom-call(f32[8,8,128]{2,1,0:T(8,128)} %v_hbm.1, f32[8,8,128]{2,1,0:T(8,128)} %c_hbm.1, s32[1,128]{1,0:T(1,128)} %bitcast.6, s32[1,1]{1,0:T(1,128)S(6)} %copy.13.count_ref, s32[64,128]{1,0:T(8,128)} %bitcast.4, ...), custom_call_target="tpu_custom_call" | custom-call | tf_op jit(solution)/shard_map/pallas_call | solution.py:322
  21.4 1.5 %shard_map.120 = (f32[8,8,128]{2,1,0:T(8,128)}, f32[8,8,128]{2,1,0:T(8,128)}, f32[7,64]{1,0:T(8,128)}, f32[64,64]{1,0:T(8,128)}, f32[1,64]{1,0:T(1,128)}) custom-call(f32[8,8,128]{2,1,0:T(8,128)} %get-tuple-element.15.refs_0_, f32[8,8,128]{2,1,0:T(8,128)} %get-tuple-element.16.refs_1_, f32[7,64]{1,0:T(8,128)} %get-tuple-element.17.refs_2_, ...), custom_call_target="tpu_custom_call" | custom-call | tf_op jit(solution)/shard_map/pallas_call | solution.py:360
